TPU v7x, 32 devices: a whole 2x2x4 slice. The times are simulated.
32 devices in a mesh: rep: 2 (over x), grp: 8 (over z, y), loc: 2 (over core).
Axes of the slice: x: 2, y: 2, z: 4, core: 2. Of those that a mesh axis runs over, the one named last changes fastest.
Arguments:
- tokens: bfloat16 [4096, 3584], P(('rep', 'grp', 'loc')), parts along dimension 0, may hold values from -6 to 6
- norm_gain: float32 [3584], replicated, may hold values from 0.5 to 1.5
- gate_weight: bfloat16 [8, 3584, 1024], P('grp', 'loc'), may hold values from -0.09375 to 0.09375
- up_weight: bfloat16 [8, 3584, 1024], P('grp', 'loc'), may hold values from -0.09375 to 0.09375
- down_weight: bfloat16 [8, 1024, 3584], P('grp', None, 'loc'), may hold values from -0.1875 to 0.1875
- expert_ids: int32 [4096, 4], P(('rep', 'grp', 'loc')), parts along dimension 0, may hold values from 0 to 7, as said below
- numerators: int32 [4096, 4], P(('rep', 'grp', 'loc')), parts along dimension 0, may hold values from 1 to 128
Outputs:
- moe_out: bfloat16 [4096, 3584], P(('rep', 'grp', 'loc')), parts along dimension 0
There are 2 independent parts, one for each index of `rep`. A program takes and returns all parts, laid end to end along the dimension named above; an argument that names none is the same for every part. Nothing has to cross between parts.
Inputs may be any that keep to these rules, and one draw needn't show every extreme that they name: `expert_ids`: expert e lies in group e // 1. Each token names 4 different experts, one in each of four different groups. In each aligned block of 128 tokens every group is named by exactly half of the tokens, no expert is named by more than 64 tokens, and some expert is named by exactly 64; some experts are named by 64 tokens of every block.
All inputs are finite; a program needn't handle non-finite values.
Results may differ from a plain program's by a relative error of at most 0.015.
Values may be sent and summed in bfloat16 or wider, within the bound.
A program may use at most 64 MiB of HBM per device.

v0:
```python
import jax
import jax.numpy as jnp
from jax import lax
from jax.sharding import PartitionSpec as P


def local(tokens, norm_gain, gate_weight, up_weight, down_weight, expert_ids, numerators):
    tok_count, width = tokens.shape
    chosen = expert_ids.shape[1]
    experts = lax.axis_size("grp")
    halves = lax.axis_size("loc")
    half_width = width // halves
    capacity = tok_count // 2 - experts // 32 * (23 * tok_count // 64)
    values = tokens.astype(jnp.float32)
    norm_scale = lax.rsqrt(jnp.mean(values * values, axis=-1, keepdims=True) + 1e-06)
    normed = (values * norm_scale * norm_gain).astype(jnp.bfloat16)
    flat_ids = expert_ids.reshape(-1)
    onehot = (flat_ids[:, None] == jnp.arange(experts, dtype=jnp.int32)[None, :]).astype(jnp.int32)
    slot_rank = jnp.sum((jnp.cumsum(onehot, axis=0) - 1) * onehot, axis=1)
    target = (flat_ids * capacity + slot_rank).reshape(tok_count, chosen)
    placed = (
        target[:, :, None] == jnp.arange(experts * capacity, dtype=jnp.int32)[None, None, :]
    ).astype(jnp.float32)
    select = jnp.sum(placed, axis=1).astype(jnp.bfloat16).reshape(tok_count, experts, capacity)
    weights = numerators.astype(jnp.float32) / 128.0
    combine = (
        jnp.sum(placed * weights[:, :, None], axis=1)
        .astype(jnp.bfloat16)
        .reshape(tok_count, experts, capacity)
    )
    feature_halves = normed.reshape(tok_count, halves, half_width)
    outgoing = jnp.einsum(
        "tec,thf->ehcf", select, feature_halves, preferred_element_type=jnp.float32
    ).astype(jnp.bfloat16)
    arrived = lax.all_to_all(
        outgoing.reshape(experts * halves, capacity, half_width),
        ("grp", "loc"),
        split_axis=0,
        concat_axis=0,
        tiled=True,
    )
    expert_input = arrived.reshape(-1, half_width)
    gate_part = jnp.dot(expert_input, gate_weight[0], preferred_element_type=jnp.float32)
    up_part = jnp.dot(expert_input, up_weight[0], preferred_element_type=jnp.float32)
    down_local = down_weight[0]
    gate_sum, up_sum = (
        lax.psum(gate_part.astype(jnp.bfloat16), "loc").astype(jnp.float32),
        lax.psum(up_part.astype(jnp.bfloat16), "loc").astype(jnp.float32),
    )
    hidden_all = (jax.nn.silu(gate_sum) * up_sum).astype(jnp.bfloat16)
    expert_out = jnp.dot(hidden_all, down_local, preferred_element_type=jnp.float32)
    expert_out = expert_out.astype(jnp.bfloat16)
    returned = lax.all_to_all(
        expert_out.reshape(experts * halves, capacity, half_width),
        ("grp", "loc"),
        split_axis=0,
        concat_axis=0,
        tiled=True,
    ).reshape(experts, halves, capacity, half_width)
    mixed = jnp.einsum("tec,ehcf->thf", combine, returned, preferred_element_type=jnp.float32)
    return mixed.reshape(tok_count, width).astype(jnp.bfloat16)


def solution(mesh):
    in_specs = (
        P(("rep", "grp", "loc"), None),
        P(),
        P("grp", "loc", None),
        P("grp", "loc", None),
        P("grp", None, "loc"),
        P(("rep", "grp", "loc"), None),
        P(("rep", "grp", "loc"), None),
    )
    out_specs = P(("rep", "grp", "loc"), None)
    return jax.shard_map(local, mesh=mesh, in_specs=in_specs, out_specs=out_specs, check_vma=False)
```

profile of v0, /device:TPU:13, one launch (start us, length us, event | category | flops | bytes accessed | tf_op | source)
XLA Modules:
  0.0 266.9 jit_solution(13242521310978403542)
XLA Ops:
  6.5 0.0 all-reduce.3.cloned.1.call-start
  6.5 0.8 copy.40
  7.3 0.1 eq.42
  7.4 0.1 eq.38
  7.5 1.4 fusion.20
  9.0 0.7 convert_multiply_fusion.3
  9.7 1.1 reduce-window.6
  10.8 0.2 slice_reduce_fusion
  11.1 0.1 fusion.24
  11.2 0.1 reduce_sum.39
  11.3 0.1 copy.42
  11.4 0.7 multiply_add_fusion
  12.1 0.2 convert_reduce_fusion
  12.3 0.1 copy.44
  12.4 1.5 fusion.22
  13.9 0.2 reshape.66
  14.1 1.1 fusion.11
  15.2 0.4 copy.46
  15.6 0.0 copy-start
  15.6 87.6 %all_to_all.10 = bf16[16,64,1792]{2,1,0:T(8,128)(2,1)S(1)} all-to-all(bf16[16,64,1792]{2,1,0:T(8,128)(2,1)S(1)} %bitcast.44), channel_id=1, replica_groups=mesh['rep'=2,'grp'=8,'loc'=2] {'grp','loc'}, dimensions={0} | all-to-all | bytes 7340032 | tf_op jit(solution)/shard_map/all_to_all | solution.py:35
  103.2 0.0 copy-done
  103.2 5.2 %fusion.17 = bf16[1024,1024]{1,0:T(8,128)(2,1)} fusion(bf16[1024,1792]{1,0:T(8,128)(2,1)S(1)} %bitcast.48, bf16[1,1792,1024]{2,1,0:T(8,128)(2,1)S(1)} %copy-done), kind=kOutput, calls=%fused_computation.22 | convolution fusion | flops 3759144960 | bytes 9437184 | tf_op jit(solution)/shard_map/dot_general | solution.py:44
  108.5 5.2 %fusion.14 = bf16[1024,1024]{1,0:T(8,128)(2,1)} fusion(bf16[1024,1792]{1,0:T(8,128)(2,1)S(1)} %bitcast.49, bf16[1,1792,1024]{2,1,0:T(8,128)(2,1)S(1)} %copy-done.1), kind=kOutput, calls=%fused_computation.21 | convolution fusion | flops 3759144960 | bytes 9437184 | tf_op jit(solution)/shard_map/dot_general | solution.py:43
  113.6 0.0 all-reduce.3.cloned.1.call-update
  113.7 29.2 %all-reduce.3.cloned.1.call-done = (bf16[1024,1024]{1,0:T(8,128)(2,1)}, bf16[1024,1024]{1,0:T(8,128)(2,1)}) async-done(((bf16[1024,1024]{1,0:T(8,128)(2,1)}, bf16[1024,1024]{1,0:T(8,128)(2,1)}), (bf16[1024,1024]{1,0:T(8,128)(2,1)}, bf16[1024,1024]{1,0:T(8,128)(2,1)})) %all-reduce.3.cloned.1.call-update) | async-done | bytes 4194320 | tf_op jit(solution)/shard_map/psum | solution.py:48
  142.9 9.9 %convolution_convert_fusion.1 = bf16[1024,1792]{1,0:T(8,128)(2,1)} fusion(bf16[1,1024,1792]{2,1,0:T(8,128)(2,1)} %param.11, bf16[1024,1024]{1,0:T(8,128)(2,1)} %get-tuple-element.7, bf16[1024,1024]{1,0:T(8,128)(2,1)} %get-tuple-element.8), kind=kOutput, calls=%fused_computation.10 | convolution fusion | flops 3768320000 | bytes 11534336 | tf_op jit(solution)/shard_map/dot_general | solution.py:51
  152.7 5.9 %all-to-all-start.1 = ((bf16[16,64,1792]{2,1,0:T(8,128)(2,1)}), bf16[16,64,1792]{2,1,0:T(8,128)(2,1)}, u32[]{:S(2)}, u32[]{:S(2)}) async-start(bf16[16,64,1792]{2,1,0:T(8,128)(2,1)} %bitcast.47), calls=%async_computation.1 | async-start | bytes 7340032 | tf_op jit(solution)/shard_map/all_to_all | solution.py:53
  158.7 0.1 copy.43
  158.8 81.1 %all-to-all-done.1 = bf16[16,64,1792]{2,1,0:T(8,128)(2,1)} async-done(((bf16[16,64,1792]{2,1,0:T(8,128)(2,1)}), bf16[16,64,1792]{2,1,0:T(8,128)(2,1)}, u32[]{:S(2)}, u32[]{:S(2)}) %all-to-all-start.1) | async-done | bytes 3670048 | tf_op jit(solution)/shard_map/all_to_all | solution.py:53
  239.9 7.6 %copy.54 = bf16[8,2,64,1792]{3,1,2,0:T(2,128)(2,1)} copy(bf16[8,2,64,1792]{3,2,1,0:T(8,128)(2,1)} %bitcast.13) | data formatting | bytes 7340032 | tf_op jit(solution)/shard_map/reshape | solution.py:59
  247.5 8.8 %dot_general.24 = bf16[3584,64,8]{0,1,2:T(8,128)(2,1)} reshape(bf16[2,1792,64,8]{1,0,2,3:T(2,128)(2,1)} %bitcast.45) | data formatting | bytes 7340032 | tf_op jit(solution)/shard_map/tec,ehcf->thf/dot_general | solution.py:60
  256.4 3.6 %fusion = bf16[128,3584]{1,0:T(8,128)(2,1)} fusion(bf16[128,8,64]{0,2,1:T(8,128)(2,1)S(1)} %bitcast.51, bf16[3584,64,8]{0,1,2:T(8,128)(2,1)} %dot_general.24), kind=kOutput, calls=%fused_computation.3 | convolution fusion | flops 470220800 | bytes 4718592 | tf_op jit(solution)/shard_map/tec,ehcf->thf/dot_general | solution.py:60
  (6 shorter events, 0.1 us)
Async XLA Ops:
  6.5 136.4 %all-reduce.3.cloned.1.call-start = ((), (), s32[]{:S(2)}) async-start(), calls=%async_computation.2 | async-start | bytes 8388608 | tf_op jit(solution)/shard_map/psum | solution.py:48
  15.6 87.6 %copy-start = (bf16[1,1792,1024]{2,1,0:T(8,128)(2,1)S(1)}, bf16[1,1792,1024]{2,1,0:T(8,128)(2,1)}, u32[]{:S(2)}) copy-start(bf16[1,1792,1024]{2,1,0:T(8,128)(2,1)} %param.10) | copy-start | bytes 11010052
  103.2 5.2 %copy-start.1 = (bf16[1,1792,1024]{2,1,0:T(8,128)(2,1)S(1)}, bf16[1,1792,1024]{2,1,0:T(8,128)(2,1)}, u32[]{:S(2)}) copy-start(bf16[1,1792,1024]{2,1,0:T(8,128)(2,1)} %param.9) | copy-start | bytes 11010052
  152.7 87.1 %all-to-all-start.1 = ((bf16[16,64,1792]{2,1,0:T(8,128)(2,1)}), bf16[16,64,1792]{2,1,0:T(8,128)(2,1)}, u32[]{:S(2)}, u32[]{:S(2)}) async-start(bf16[16,64,1792]{2,1,0:T(8,128)(2,1)} %bitcast.47), calls=%async_computation.1 | async-start | bytes 7340032 | tf_op jit(solution)/shard_map/all_to_all | solution.py:53
Sparse Core Ops, SparseCore 0:
  113.8 29.0 all-reduce.2
where the time goes:
time: 267 us
  waiting for transfers between devices  110 us (41%)
  blocking collectives  87.6 us (33%)
  matrix products  25 us (9%)
  local copies, waits for them, and re-layouts  18.7 us (7%)
  between operations  13.5 us (5%)
  starting transfers between devices  5.91 us (2%)
  other arithmetic  5.83 us (2%)
    all_to_all x1, blocking collectives, local(): lax.all_to_all(outgoing.reshape(experts * halves, capacity, half_width),...  87.6 us
    all_to_all x1, waiting for transfers between devices, local(): lax.all_to_all(expert_out.reshape(experts * halves, capacity, half_width)...  81.1 us
    psum x1, waiting for transfers between devices, local(): lax.psum(up_part.astype(jnp.bfloat16), 'loc').astype(jnp.float32)  29.2 us
    dot_general x1, matrix products, local(): jnp.dot(hidden_all, down_local, preferred_element_type=jnp.float32)  9.86 us
    dot_general x1, local copies, waits for them, and re-layouts, local(): jnp.einsum('tec,ehcf->thf', combine, returned, preferred_element_type=jnp...  8.84 us
    reshape x1, local copies, waits for them, and re-layouts, local(): returned = lax.all_to_all(expert_out.reshape(experts * halves, capacity,...  7.65 us
    all_to_all x1, starting transfers between devices, local(): lax.all_to_all(expert_out.reshape(experts * halves, capacity, half_width)...  5.91 us
  transfers between devices with their start and end apart: 2, of which 2 were waited for; matrix products, arithmetic and copies ran while one was open for 0% of the time, Pallas kernels for 0%

commit v1 on v0

--- a/solution.py
+++ b/solution.py
@@ -1,6 +1,10 @@
+import functools
+
 import jax
 import jax.numpy as jnp
 from jax import lax
+from jax.experimental import pallas as pl
+from jax.experimental.pallas import tpu as pltpu
 from jax.sharding import PartitionSpec as P
 
 
@@ -61,6 +65,360 @@
     return mixed.reshape(tok_count, width).astype(jnp.bfloat16)
 
 
+def chain_kernel(
+    lanes, steps, cap,
+    tok_ref, gain_ref, ids_ref, num_ref, gate_hbm, up_hbm, down_hbm, out_ref,
+    gate_w, up_w, down_w, stage, gathered, meta, cross, rows, part, part_in, made, back, total, total_in, last, last_in,
+    weight_sem, pair_send, pair_recv, pair_meta_send, pair_meta_recv, hop_send, hop_recv, meta_send, meta_recv,
+    cross_send, cross_recv, part_send, part_recv, back_send, back_recv, sum_send, sum_recv, last_send, last_recv,
+):
+    tok_count, width = tok_ref.shape
+    half_width = width // 2
+    hidden_width = gate_w.shape[1]
+    experts = lanes * steps
+    group = lax.axis_index("grp")
+    core = lax.axis_index("loc")
+    place = group // lanes
+    lane = group % lanes
+    other_core = 1 - core
+    other_lane = place * lanes + 1 - lane
+    left, right = group - lanes, group + lanes
+    has_left, has_right = place > 0, place < steps - 1
+    mesh_id = pl.DeviceIdType.MESH
+
+    def remote(src, dst, send, recv, target):
+        return pltpu.make_async_remote_copy(
+            src_ref=src, dst_ref=dst, send_sem=send, recv_sem=recv, device_id=target, device_id_type=mesh_id
+        )
+
+    weight_copies = [
+        pltpu.make_async_copy(src.at[0], dst, weight_sem.at[k])
+        for k, (src, dst) in enumerate(((gate_hbm, gate_w), (up_hbm, up_w), (down_hbm, down_w)))
+    ]
+    for copy in weight_copies:
+        copy.start()
+
+    barrier = pltpu.get_barrier_semaphore()
+    pl.semaphore_signal(barrier, inc=1, device_id={"loc": other_core}, device_id_type=mesh_id)
+    pl.semaphore_signal(barrier, inc=1, device_id={"grp": other_lane}, device_id_type=mesh_id)
+
+    @pl.when(has_left)
+    def _():
+        pl.semaphore_signal(barrier, inc=1, device_id={"grp": left}, device_id_type=mesh_id)
+
+    @pl.when(has_right)
+    def _():
+        pl.semaphore_signal(barrier, inc=1, device_id={"grp": right}, device_id_type=mesh_id)
+
+    expert_row = lax.broadcasted_iota(jnp.int32, (experts, tok_count), 0)
+    named = jnp.zeros((experts, tok_count), jnp.float32)
+    weight = jnp.zeros((experts, tok_count), jnp.float32)
+    for k in range(ids_ref.shape[0]):
+        hit = ids_ref[k : k + 1, :] == expert_row
+        named = named + jnp.where(hit, 1.0, 0.0)
+        weight = weight + jnp.where(hit, num_ref[k : k + 1, :].astype(jnp.float32) / 128.0, 0.0)
+    earlier = lax.broadcasted_iota(jnp.int32, (tok_count, tok_count), 0) < lax.broadcasted_iota(
+        jnp.int32, (tok_count, tok_count), 1
+    )
+    slot = jnp.dot(
+        named.astype(jnp.bfloat16),
+        jnp.where(earlier, 1.0, 0.0).astype(jnp.bfloat16),
+        preferred_element_type=jnp.float32,
+    )
+    meta[place, core, 0:experts, :] = jnp.where(named > 0.5, slot, -1.0)
+    meta[place, core, experts : 2 * experts, :] = weight
+
+    values = tok_ref[...].astype(jnp.float32)
+    scale = lax.rsqrt(jnp.mean(values * values, axis=-1, keepdims=True) + 1e-06)
+
+    def normed(which):
+        cols = pl.ds(pl.multiple_of(which * half_width, 128), half_width)
+        return (tok_ref[:, cols].astype(jnp.float32) * scale * gain_ref[:, cols]).astype(jnp.bfloat16)
+
+    stage[...] = normed(other_core)
+    pl.semaphore_wait(barrier, 2 + has_left.astype(jnp.int32) + has_right.astype(jnp.int32))
+    own = (place, core)
+    pair_copies = [
+        remote(stage, gathered.at[own], pair_send, pair_recv, {"loc": other_core}),
+        remote(meta.at[own], meta.at[own], pair_meta_send, pair_meta_recv, {"loc": other_core}),
+    ]
+    for copy in pair_copies:
+        copy.start()
+    gathered[place, core] = normed(core)
+    for copy in pair_copies:
+        copy.wait_send()
+
+    def hop(b, h, side):
+        target = {"grp": (left, right)[side]}
+        return (
+            remote(gathered.at[b, h], gathered.at[b, h], hop_send.at[side, b, h], hop_recv.at[b, h], target),
+            remote(meta.at[b, h], meta.at[b, h], meta_send.at[side, b, h], meta_recv.at[b, h], target),
+        )
+
+    def start_hop(b, h, side):
+        for copy in hop(b, h, side):
+            copy.start()
+
+    def forward(i):
+        h, d = i // steps, i % steps
+
+        @pl.when(d == 0)
+        def _():
+            @pl.when(h != core)
+            def _():
+                got = (place, other_core)
+                remote(stage, gathered.at[got], pair_send, pair_recv, {"loc": other_core}).wait_recv()
+                remote(meta.at[got], meta.at[got], pair_meta_send, pair_meta_recv, {"loc": other_core}).wait_recv()
+
+            @pl.when(has_left)
+            def _():
+                start_hop(place, h, 0)
+
+            @pl.when(has_right)
+            def _():
+                start_hop(place, h, 1)
+
+        @pl.when((d > 0) & (place - d >= 0))
+        def _():
+            for copy in hop(place - d, h, 1):
+                copy.wait_recv()
+
+            @pl.when(has_right)
+            def _():
+                start_hop(place - d, h, 1)
+
+        @pl.when((d > 0) & (place + d < steps))
+        def _():
+            for copy in hop(place + d, h, 0):
+                copy.wait_recv()
+
+            @pl.when(has_left)
+            def _():
+                start_hop(place + d, h, 0)
+
+    def chunk(i):
+        h, j = i // steps, i % steps
+        near = jnp.minimum(place, steps - 1 - place)
+        both = j <= 2 * near
+        d = jnp.where(both, (j + 1) // 2, j - near)
+        up = jnp.where(both, j % 2 == 0, place < steps - 1 - place)
+        return jnp.where(up, place + d, place - d), h
+
+    slot_row = lax.broadcasted_iota(jnp.int32, (cap, tok_count), 0).astype(jnp.float32)
+
+    def table(b, h, expert):
+        return meta[b, h, pl.ds(expert, 1), :] == slot_row
+
+    def weighted(b, h, expert):
+        return jnp.where(table(b, h, expert), meta[b, h, pl.ds(experts + expert, 1), :], 0.0).astype(jnp.bfloat16)
+
+    def pick(b, h, expert):
+        chosen = jnp.where(table(b, h, expert), 1.0, 0.0).astype(jnp.bfloat16)
+        return jnp.dot(chosen, gathered[b, h], preferred_element_type=jnp.float32).astype(jnp.bfloat16)
+
+    def cross_copy(b, h):
+        return remote(
+            cross.at[b, h], rows.at[b, h, pl.ds(cap, cap)], cross_send.at[b, h], cross_recv.at[b, h], {"grp": other_lane}
+        )
+
+    def part_copy(b, h):
+        return remote(part.at[b, h], part_in.at[b, h], part_send.at[b, h], part_recv.at[b, h], {"loc": other_core})
+
+    def back_copy(b, h):
+        return remote(
+            made.at[b, h, pl.ds(cap, cap)], back.at[b, h], back_send.at[b, h], back_recv.at[b, h], {"grp": other_lane}
+        )
+
+    def sum_copy(b, h, side):
+        return remote(
+            total.at[b, h],
+            total_in.at[side, b, h],
+            sum_send.at[b, h],
+            sum_recv.at[side, b, h],
+            {"grp": (left, right)[side]},
+        )
+
+    def select(b, h):
+        cross[b, h] = pick(b, h, other_lane)
+        cross_copy(b, h).start()
+        rows[b, h, 0:cap, :] = pick(b, h, group)
+
+    def experts_of(b, h):
+        cross_copy(b, h).wait_recv()
+        for k, w in enumerate((gate_w, up_w)):
+            part[b, h, :, k * hidden_width : (k + 1) * hidden_width] = jnp.dot(
+                rows[b, h], w[...], preferred_element_type=jnp.float32
+            ).astype(jnp.bfloat16)
+        part_copy(b, h).start()
+        part_copy(b, h).wait_recv()
+        both = part[b, h].astype(jnp.float32) + part_in[b, h].astype(jnp.float32)
+        gate_sum, up_sum = both[:, :hidden_width], both[:, hidden_width:]
+        hidden = (gate_sum / (1.0 + jnp.exp(-gate_sum)) * up_sum).astype(jnp.bfloat16)
+        made[b, h] = jnp.dot(hidden, down_w[...], preferred_element_type=jnp.float32).astype(jnp.bfloat16)
+        back_copy(b, h).start()
+
+    def combine(b, h):
+        back_copy(b, h).wait_recv()
+        dims = (((0,), (0,)), ((), ()))
+        total[b, h] = (
+            lax.dot_general(weighted(b, h, group), made[b, h, 0:cap, :], dims, preferred_element_type=jnp.float32)
+            + lax.dot_general(weighted(b, h, other_lane), back[b, h], dims, preferred_element_type=jnp.float32)
+        ).astype(jnp.bfloat16)
+
+        @pl.when((b > place) & jnp.logical_not(has_left))
+        def _():
+            sum_copy(b, h, 1).start()
+
+        @pl.when((b < place) & jnp.logical_not(has_right))
+        def _():
+            sum_copy(b, h, 0).start()
+
+    def add_in(b, h, side):
+        sum_copy(b, h, side).wait_recv()
+        total[b, h] = (total[b, h].astype(jnp.float32) + total_in[side, b, h].astype(jnp.float32)).astype(jnp.bfloat16)
+
+    def reduce_step(i):
+        for h in range(2):
+            going_right = i - h * steps - 2 * place
+            going_left = steps - 1 - (i - h * steps - 2 * (steps - 1 - place))
+
+            @pl.when(has_left & (going_right > place) & (going_right < steps))
+            def _():
+                add_in(going_right, h, 1)
+                sum_copy(going_right, h, 1).start()
+
+            @pl.when(has_right & (going_left < place) & (going_left >= 0))
+            def _():
+                add_in(going_left, h, 0)
+                sum_copy(going_left, h, 0).start()
+
+    def body(i, carry):
+        @pl.when(i < 2 * steps)
+        def _():
+            forward(i)
+            select(*chunk(i))
+
+        reduce_step(i)
+
+        @pl.when((i >= 1) & (i <= 2 * steps))
+        def _():
+            combine(*chunk(i - 1))
+
+        @pl.when(i == 0)
+        def _():
+            for copy in weight_copies:
+                copy.wait()
+
+        @pl.when(i < 2 * steps)
+        def _():
+            experts_of(*chunk(i))
+
+        return carry
+
+    lax.fori_loop(0, max(4 * steps - 4, 2 * steps + 1), body, 0)
+
+    def finish(h):
+        @pl.when(has_left)
+        def _():
+            add_in(place, h, 1)
+
+        @pl.when(has_right)
+        def _():
+            add_in(place, h, 0)
+
+    last_copy = remote(last, last_in, last_send, last_recv, {"loc": other_core})
+    for h in range(2):
+        finish(h)
+
+        @pl.when(h != core)
+        def _():
+            last[...] = total[place, h]
+            last_copy.start()
+
+        @pl.when(h == core)
+        def _():
+            out_ref[:, pl.ds(pl.multiple_of(core * half_width, 128), half_width)] = total[place, h]
+
+    last_copy.wait()
+    out_ref[:, pl.ds(pl.multiple_of(other_core * half_width, 128), half_width)] = last_in[...]
+
+    def drain(i, carry):
+        b, h = i // 2, i % 2
+
+        @pl.when((b <= place) & has_right)
+        def _():
+            for copy in hop(b, h, 1):
+                copy.wait_send()
+
+        @pl.when((b >= place) & has_left)
+        def _():
+            for copy in hop(b, h, 0):
+                copy.wait_send()
+
+        cross_copy(b, h).wait_send()
+        part_copy(b, h).wait_send()
+        back_copy(b, h).wait_send()
+
+        @pl.when(b != place)
+        def _():
+            sum_copy(b, h, 0).wait_send()
+
+        return carry
+
+    lax.fori_loop(0, 2 * steps, drain, 0)
+
+
+def chained(tokens, norm_gain, gate_weight, up_weight, down_weight, expert_ids, numerators):
+    tok_count, width = tokens.shape
+    experts = lax.axis_size("grp")
+    half_width = width // 2
+    hidden_width = gate_weight.shape[2]
+    lanes = 2
+    steps = experts // lanes
+    cap = capacity_of(tok_count, experts)
+    bf = jnp.bfloat16
+    dma = pltpu.SemaphoreType.DMA
+    vmem = pl.BlockSpec(memory_space=pltpu.VMEM)
+    hbm = pl.BlockSpec(memory_space=pl.ANY)
+    return pl.pallas_call(
+        functools.partial(chain_kernel, lanes, steps, cap),
+        out_shape=jax.ShapeDtypeStruct((tok_count, width), bf),
+        in_specs=[vmem, vmem, vmem, vmem, hbm, hbm, hbm],
+        out_specs=vmem,
+        scratch_shapes=[
+            pltpu.VMEM((half_width, hidden_width), bf),
+            pltpu.VMEM((half_width, hidden_width), bf),
+            pltpu.VMEM((hidden_width, half_width), bf),
+            pltpu.VMEM((tok_count, half_width), bf),
+            pltpu.VMEM((steps, 2, tok_count, half_width), bf),
+            pltpu.VMEM((steps, 2, 2 * experts, tok_count), jnp.float32),
+            pltpu.VMEM((steps, 2, cap, half_width), bf),
+            pltpu.VMEM((steps, 2, 2 * cap, half_width), bf),
+            pltpu.VMEM((steps, 2, 2 * cap, 2 * hidden_width), bf),
+            pltpu.VMEM((steps, 2, 2 * cap, 2 * hidden_width), bf),
+            pltpu.VMEM((steps, 2, 2 * cap, half_width), bf),
+            pltpu.VMEM((steps, 2, cap, half_width), bf),
+            pltpu.VMEM((steps, 2, tok_count, half_width), bf),
+            pltpu.VMEM((2, steps, 2, tok_count, half_width), bf),
+            pltpu.VMEM((tok_count, half_width), bf),
+            pltpu.VMEM((tok_count, half_width), bf),
+            dma((3,)),
+            dma, dma, dma, dma,
+            dma((2, steps, 2)), dma((steps, 2)), dma((2, steps, 2)), dma((steps, 2)),
+            dma((steps, 2)), dma((steps, 2)), dma((steps, 2)), dma((steps, 2)),
+            dma((steps, 2)), dma((steps, 2)), dma((steps, 2)), dma((2, steps, 2)),
+            dma, dma,
+        ],
+        compiler_params=pltpu.CompilerParams(
+            collective_id=0, has_side_effects=True, vmem_limit_bytes=60 * 1024 * 1024
+        ),
+    )(tokens, norm_gain[None, :], expert_ids.T, numerators.T, gate_weight, up_weight, down_weight)
+
+
+def capacity_of(tok_count, experts):
+    return tok_count // 2 - experts // 32 * (23 * tok_count // 64)
+
+
 def solution(mesh):
     in_specs = (
         P(("rep", "grp", "loc"), None),
@@ -72,4 +430,13 @@
         P(("rep", "grp", "loc"), None),
     )
     out_specs = P(("rep", "grp", "loc"), None)
-    return jax.shard_map(local, mesh=mesh, in_specs=in_specs, out_specs=out_specs, check_vma=False)
+    experts, halves = mesh.shape["grp"], mesh.shape["loc"]
+
+    def run(tokens, *rest):
+        tok_count = tokens.shape[0] // mesh.size
+        whole_tiles = capacity_of(tok_count, experts) % 16 == 0 and experts % 8 == 0 and halves == 2
+        return jax.shard_map(
+            chained if whole_tiles else local, mesh=mesh, in_specs=in_specs, out_specs=out_specs, check_vma=False
+        )(tokens, *rest)
+
+    return run

time: 267 us -> 175 us (0.66)
  the two profiles are of different devices: /device:TPU:13 before, /device:TPU:0 now
where the time goes in v1:
time: 175 us
  Pallas kernels  171 us (98%)
  local copies, waits for them, and re-layouts  3.49 us (2%)
    pallas_call x1, Pallas kernels, chained(): pl.pallas_call(functools.partial(chain_kernel, lanes, steps, cap), out_sh...  171 us

profile of v1, /device:TPU:0, one launch (start us, length us, event | category | flops | bytes accessed | tf_op | source)
XLA Modules:
  0.0 174.9 jit_solution(11563432546102612924)
XLA Ops:
  0.0 1.3 broadcast_in_dim.3.gain_ref
  1.3 171.4 %shard_map.73 = bf16[128,3584]{1,0:T(8,128)(2,1)} custom-call(bf16[128,3584]{1,0:T(8,128)(2,1)} %tok_ref.1, f32[1,3584]{1,0:T(1,128)} %broadcast_in_dim.3.gain_ref, s32[4,128]{1,0:T(4,128)} %bitcast.2, s32[4,128]{1,0:T(4,128)} %bitcast.3, bf16[1,1792,1024]{2,1,0:T(8,128)(2,1)} %gate_hbm.1, bf16[1,1792,1024]{2,1,0:T(8,128)(2,1)} %up_hbm.1, ...), custom_call_target="tpu_custom_call" | custom-call | tf_op jit(solution)/shard_map/pallas_call | solution.py:383
  172.8 2.2 %copy.9 = bf16[128,3584]{1,0:T(8,128)(2,1)} copy(bf16[128,3584]{1,0:T(8,128)(2,1)} %shard_map.73) | data formatting | bytes 1835008

commit v2 on v1

--- a/solution.py
+++ b/solution.py
@@ -76,6 +76,7 @@
     half_width = width // 2
     hidden_width = gate_w.shape[1]
     experts = lanes * steps
+    half_tok = tok_count // 2
     group = lax.axis_index("grp")
     core = lax.axis_index("loc")
     place = group // lanes
@@ -147,6 +148,9 @@
     gathered[place, core] = normed(core)
     for copy in pair_copies:
         copy.wait_send()
+    got = (place, other_core)
+    remote(stage, gathered.at[got], pair_send, pair_recv, {"loc": other_core}).wait_recv()
+    remote(meta.at[got], meta.at[got], pair_meta_send, pair_meta_recv, {"loc": other_core}).wait_recv()
 
     def hop(b, h, side):
         target = {"grp": (left, right)[side]}
@@ -159,45 +163,29 @@
         for copy in hop(b, h, side):
             copy.start()
 
+    def forward_one(i, upstream, sign, side, has_next):
+        first = i <= upstream
+        d = jnp.where(first, i, 2 * upstream + 1 - i)
+        b, h = place + sign * d, jnp.where(first, 0, 1)
+
+        @pl.when(d >= 0)
+        def _():
+            @pl.when(d > 0)
+            def _():
+                for copy in hop(b, h, side):
+                    copy.wait_recv()
+
+            @pl.when(has_next)
+            def _():
+                start_hop(b, h, side)
+
     def forward(i):
-        h, d = i // steps, i % steps
-
-        @pl.when(d == 0)
-        def _():
-            @pl.when(h != core)
-            def _():
-                got = (place, other_core)
-                remote(stage, gathered.at[got], pair_send, pair_recv, {"loc": other_core}).wait_recv()
-                remote(meta.at[got], meta.at[got], pair_meta_send, pair_meta_recv, {"loc": other_core}).wait_recv()
-
-            @pl.when(has_left)
-            def _():
-                start_hop(place, h, 0)
-
-            @pl.when(has_right)
-            def _():
-                start_hop(place, h, 1)
-
-        @pl.when((d > 0) & (place - d >= 0))
-        def _():
-            for copy in hop(place - d, h, 1):
-                copy.wait_recv()
-
-            @pl.when(has_right)
-            def _():
-                start_hop(place - d, h, 1)
-
-        @pl.when((d > 0) & (place + d < steps))
-        def _():
-            for copy in hop(place + d, h, 0):
-                copy.wait_recv()
-
-            @pl.when(has_left)
-            def _():
-                start_hop(place + d, h, 0)
+        forward_one(i, steps - 1 - place, 1, 0, has_left)
+        forward_one(i, place, -1, 1, has_right)
 
     def chunk(i):
-        h, j = i // steps, i % steps
+        h = i // steps
+        j = jnp.where(h == 0, i, 2 * steps - 1 - i)
         near = jnp.minimum(place, steps - 1 - place)
         both = j <= 2 * near
         d = jnp.where(both, (j + 1) // 2, j - near)
@@ -229,12 +217,13 @@
             made.at[b, h, pl.ds(cap, cap)], back.at[b, h], back_send.at[b, h], back_recv.at[b, h], {"grp": other_lane}
         )
 
-    def sum_copy(b, h, side):
+    def sum_copy(b, h, side, p):
+        at = pl.ds(p * half_tok, half_tok)
         return remote(
-            total.at[b, h],
-            total_in.at[side, b, h],
-            sum_send.at[b, h],
-            sum_recv.at[side, b, h],
+            total.at[b, h, at],
+            total_in.at[side, b, h, at],
+            sum_send.at[b, h, p],
+            sum_recv.at[side, b, h, p],
             {"grp": (left, right)[side]},
         )
 
@@ -243,13 +232,15 @@
         cross_copy(b, h).start()
         rows[b, h, 0:cap, :] = pick(b, h, group)
 
-    def experts_of(b, h):
+    def gate_up(b, h):
         cross_copy(b, h).wait_recv()
         for k, w in enumerate((gate_w, up_w)):
             part[b, h, :, k * hidden_width : (k + 1) * hidden_width] = jnp.dot(
                 rows[b, h], w[...], preferred_element_type=jnp.float32
             ).astype(jnp.bfloat16)
         part_copy(b, h).start()
+
+    def down(b, h):
         part_copy(b, h).wait_recv()
         both = part[b, h].astype(jnp.float32) + part_in[b, h].astype(jnp.float32)
         gate_sum, up_sum = both[:, :hidden_width], both[:, hidden_width:]
@@ -267,30 +258,42 @@
 
         @pl.when((b > place) & jnp.logical_not(has_left))
         def _():
-            sum_copy(b, h, 1).start()
+            for p in range(2):
+                sum_copy(b, h, 1, p).start()
 
         @pl.when((b < place) & jnp.logical_not(has_right))
         def _():
-            sum_copy(b, h, 0).start()
-
-    def add_in(b, h, side):
-        sum_copy(b, h, side).wait_recv()
-        total[b, h] = (total[b, h].astype(jnp.float32) + total_in[side, b, h].astype(jnp.float32)).astype(jnp.bfloat16)
+            for p in range(2):
+                sum_copy(b, h, 0, p).start()
+
+    def add_in(b, h, side, p):
+        sum_copy(b, h, side, p).wait_recv()
+        at = pl.ds(p * half_tok, half_tok)
+        total[b, h, at] = (
+            total[b, h, at].astype(jnp.float32) + total_in[side, b, h, at].astype(jnp.float32)
+        ).astype(jnp.bfloat16)
+
+    def add_on(b, h, side):
+        for p in range(2):
+            add_in(b, h, side, p)
+            sum_copy(b, h, side, p).start()
 
     def reduce_step(i):
         for h in range(2):
-            going_right = i - h * steps - 2 * place
-            going_left = steps - 1 - (i - h * steps - 2 * (steps - 1 - place))
+            since_right = i - 2 - 2 * place
+            since_left = i - 2 - 2 * (steps - 1 - place)
+            if h == 0:
+                going_right, going_left = since_right, steps - 1 - since_left
+            else:
+                going_right, going_left = 2 * steps - 1 - since_right, since_left - steps
 
             @pl.when(has_left & (going_right > place) & (going_right < steps))
             def _():
-                add_in(going_right, h, 1)
-                sum_copy(going_right, h, 1).start()
+                add_on(going_right, h, 1)
 
             @pl.when(has_right & (going_left < place) & (going_left >= 0))
             def _():
-                add_in(going_left, h, 0)
-                sum_copy(going_left, h, 0).start()
+                add_on(going_left, h, 0)
 
     def body(i, carry):
         @pl.when(i < 2 * steps)
@@ -298,33 +301,39 @@
             forward(i)
             select(*chunk(i))
 
-        reduce_step(i)
-
-        @pl.when((i >= 1) & (i <= 2 * steps))
-        def _():
-            combine(*chunk(i - 1))
-
         @pl.when(i == 0)
         def _():
             for copy in weight_copies:
                 copy.wait()
 
-        @pl.when(i < 2 * steps)
-        def _():
-            experts_of(*chunk(i))
+        @pl.when((i >= 1) & (i <= 2 * steps))
+        def _():
+            gate_up(*chunk(i - 1))
+
+        @pl.when((i >= 2) & (i <= 2 * steps + 1))
+        def _():
+            combine(*chunk(i - 2))
+
+        reduce_step(i)
+
+        @pl.when((i >= 1) & (i <= 2 * steps))
+        def _():
+            down(*chunk(i - 1))
 
         return carry
 
-    lax.fori_loop(0, max(4 * steps - 4, 2 * steps + 1), body, 0)
+    lax.fori_loop(0, max(3 * steps - 1, 2 * steps + 2), body, 0)
 
     def finish(h):
         @pl.when(has_left)
         def _():
-            add_in(place, h, 1)
+            for p in range(2):
+                add_in(place, h, 1, p)
 
         @pl.when(has_right)
         def _():
-            add_in(place, h, 0)
+            for p in range(2):
+                add_in(place, h, 0, p)
 
     last_copy = remote(last, last_in, last_send, last_recv, {"loc": other_core})
     for h in range(2):
@@ -361,7 +370,8 @@
 
         @pl.when(b != place)
         def _():
-            sum_copy(b, h, 0).wait_send()
+            for p in range(2):
+                sum_copy(b, h, 0, p).wait_send()
 
         return carry
 
@@ -406,7 +416,7 @@
             dma, dma, dma, dma,
             dma((2, steps, 2)), dma((steps, 2)), dma((2, steps, 2)), dma((steps, 2)),
             dma((steps, 2)), dma((steps, 2)), dma((steps, 2)), dma((steps, 2)),
-            dma((steps, 2)), dma((steps, 2)), dma((steps, 2)), dma((2, steps, 2)),
+            dma((steps, 2)), dma((steps, 2)), dma((steps, 2, 2)), dma((2, steps, 2, 2)),
             dma, dma,
         ],
         compiler_params=pltpu.CompilerParams(

time: 175 us -> 130 us (0.74)
  Pallas kernels: 171 us -> 126 us
    pallas_call x1, Pallas kernels: 171 us -> 126 us  [chained(): pl.pallas_call(functools.partial(chain_kernel, lanes, steps, cap), out_sh...]
where the time goes in v2:
time: 130 us; the launch traced here: 129 us
  Pallas kernels  126 us (97%)
  local copies, waits for them, and re-layouts  3.49 us (3%)
    pallas_call x1, Pallas kernels, chained(): pl.pallas_call(functools.partial(chain_kernel, lanes, steps, cap), out_sh...  126 us

profile of v2, /device:TPU:0, one launch (start us, length us, event | category | flops | bytes accessed | tf_op | source)
XLA Modules:
  0.0 129.3 jit_solution(6232323884583939704)
XLA Ops:
  0.0 1.3 %broadcast_in_dim.3.gain_ref = f32[1,3584]{1,0:T(1,128)} reshape(f32[3584]{0:T(1024)} %param.8) | data formatting | bytes 28672 | tf_op jit(solution)/shard_map/broadcast_in_dim | solution.py:425
  1.3 125.8 %shard_map.73 = bf16[128,3584]{1,0:T(8,128)(2,1)} custom-call(bf16[128,3584]{1,0:T(8,128)(2,1)} %tok_ref.1, f32[1,3584]{1,0:T(1,128)} %broadcast_in_dim.3.gain_ref, s32[4,128]{1,0:T(4,128)} %bitcast.2, s32[4,128]{1,0:T(4,128)} %bitcast.3, bf16[1,1792,1024]{2,1,0:T(8,128)(2,1)} %gate_hbm.1, bf16[1,1792,1024]{2,1,0:T(8,128)(2,1)} %up_hbm.1, ...), custom_call_target="tpu_custom_call" | custom-call | tf_op jit(solution)/shard_map/pallas_call | solution.py:393
  127.2 2.2 %copy.9 = bf16[128,3584]{1,0:T(8,128)(2,1)} copy(bf16[128,3584]{1,0:T(8,128)(2,1)} %shard_map.73) | data formatting | bytes 1835008

commit v3 on v2

--- a/solution.py
+++ b/solution.py
@@ -134,7 +134,7 @@
 
     def normed(which):
         cols = pl.ds(pl.multiple_of(which * half_width, 128), half_width)
-        return (tok_ref[:, cols].astype(jnp.float32) * scale * gain_ref[:, cols]).astype(jnp.bfloat16)
+        return (tok_ref[:, cols].astype(jnp.float32) * scale * gain_ref[cols][None, :]).astype(jnp.bfloat16)
 
     stage[...] = normed(other_core)
     pl.semaphore_wait(barrier, 2 + has_left.astype(jnp.int32) + has_right.astype(jnp.int32))
@@ -152,36 +152,48 @@
     remote(stage, gathered.at[got], pair_send, pair_recv, {"loc": other_core}).wait_recv()
     remote(meta.at[got], meta.at[got], pair_meta_send, pair_meta_recv, {"loc": other_core}).wait_recv()
 
-    def hop(b, h, side):
+    def hop(b, h, side, p):
         target = {"grp": (left, right)[side]}
-        return (
-            remote(gathered.at[b, h], gathered.at[b, h], hop_send.at[side, b, h], hop_recv.at[b, h], target),
-            remote(meta.at[b, h], meta.at[b, h], meta_send.at[side, b, h], meta_recv.at[b, h], target),
-        )
-
-    def start_hop(b, h, side):
-        for copy in hop(b, h, side):
+        at = pl.ds(p * half_tok, half_tok)
+        chunk_rows = gathered.at[b, h, at]
+        copies = [remote(chunk_rows, chunk_rows, hop_send.at[side, b, h, p], hop_recv.at[b, h, p], target)]
+        if p == 0:
+            copies.append(
+                remote(meta.at[b, h], meta.at[b, h], meta_send.at[side, b, h], meta_recv.at[b, h], target)
+            )
+        return copies
+
+    def start_hop(b, h, side, p):
+        for copy in hop(b, h, side, p):
             copy.start()
 
-    def forward_one(i, upstream, sign, side, has_next):
+    def hop_of(i, upstream, sign):
         first = i <= upstream
         d = jnp.where(first, i, 2 * upstream + 1 - i)
-        b, h = place + sign * d, jnp.where(first, 0, 1)
-
-        @pl.when(d >= 0)
-        def _():
-            @pl.when(d > 0)
+        return d, place + sign * d, jnp.where(first, 0, 1)
+
+    def forward(i):
+        ways = ((steps - 1 - place, 1, 0, has_left), (place, -1, 1, has_right))
+        for upstream, sign, side, has_next in ways:
+            d, b, h = hop_of(i, upstream, sign)
+
+            @pl.when((d == 0) & has_next)
             def _():
-                for copy in hop(b, h, side):
-                    copy.wait_recv()
-
-            @pl.when(has_next)
-            def _():
-                start_hop(b, h, side)
-
-    def forward(i):
-        forward_one(i, steps - 1 - place, 1, 0, has_left)
-        forward_one(i, place, -1, 1, has_right)
+                for p in range(2):
+                    start_hop(b, h, side, p)
+
+        for p in range(2):
+            for upstream, sign, side, has_next in ways:
+                d, b, h = hop_of(i, upstream, sign)
+
+                @pl.when(d > 0)
+                def _():
+                    for copy in hop(b, h, side, p):
+                        copy.wait_recv()
+
+                    @pl.when(has_next)
+                    def _():
+                        start_hop(b, h, side, p)
 
     def chunk(i):
         h = i // steps
@@ -280,8 +292,8 @@
 
     def reduce_step(i):
         for h in range(2):
-            since_right = i - 2 - 2 * place
-            since_left = i - 2 - 2 * (steps - 1 - place)
+            since_right = i - 1 - 2 * place
+            since_left = i - 1 - 2 * (steps - 1 - place)
             if h == 0:
                 going_right, going_left = since_right, steps - 1 - since_left
             else:
@@ -298,31 +310,35 @@
     def body(i, carry):
         @pl.when(i < 2 * steps)
         def _():
-            forward(i)
             select(*chunk(i))
+
+        @pl.when((i >= 1) & (i <= 2 * steps))
+        def _():
+            down(*chunk(i - 1))
+
+        reduce_step(i)
 
         @pl.when(i == 0)
         def _():
             for copy in weight_copies:
                 copy.wait()
 
+        @pl.when(i < 2 * steps)
+        def _():
+            gate_up(*chunk(i))
+
+        @pl.when(i + 1 < 2 * steps)
+        def _():
+            forward(i + 1)
+
         @pl.when((i >= 1) & (i <= 2 * steps))
         def _():
-            gate_up(*chunk(i - 1))
-
-        @pl.when((i >= 2) & (i <= 2 * steps + 1))
-        def _():
-            combine(*chunk(i - 2))
-
-        reduce_step(i)
-
-        @pl.when((i >= 1) & (i <= 2 * steps))
-        def _():
-            down(*chunk(i - 1))
+            combine(*chunk(i - 1))
 
         return carry
 
-    lax.fori_loop(0, max(3 * steps - 1, 2 * steps + 2), body, 0)
+    forward(0)
+    lax.fori_loop(0, max(3 * steps - 2, 2 * steps + 1), body, 0)
 
     def finish(h):
         @pl.when(has_left)
@@ -356,13 +372,15 @@
 
         @pl.when((b <= place) & has_right)
         def _():
-            for copy in hop(b, h, 1):
-                copy.wait_send()
+            for p in range(2):
+                for copy in hop(b, h, 1, p):
+                    copy.wait_send()
 
         @pl.when((b >= place) & has_left)
         def _():
-            for copy in hop(b, h, 0):
-                copy.wait_send()
+            for p in range(2):
+                for copy in hop(b, h, 0, p):
+                    copy.wait_send()
 
         cross_copy(b, h).wait_send()
         part_copy(b, h).wait_send()
@@ -414,7 +432,7 @@
             pltpu.VMEM((tok_count, half_width), bf),
             dma((3,)),
             dma, dma, dma, dma,
-            dma((2, steps, 2)), dma((steps, 2)), dma((2, steps, 2)), dma((steps, 2)),
+            dma((2, steps, 2, 2)), dma((steps, 2, 2)), dma((2, steps, 2)), dma((steps, 2)),
             dma((steps, 2)), dma((steps, 2)), dma((steps, 2)), dma((steps, 2)),
             dma((steps, 2)), dma((steps, 2)), dma((steps, 2, 2)), dma((2, steps, 2, 2)),
             dma, dma,
@@ -422,7 +440,7 @@
         compiler_params=pltpu.CompilerParams(
             collective_id=0, has_side_effects=True, vmem_limit_bytes=60 * 1024 * 1024
         ),
-    )(tokens, norm_gain[None, :], expert_ids.T, numerators.T, gate_weight, up_weight, down_weight)
+    )(tokens, norm_gain, expert_ids.T, numerators.T, gate_weight, up_weight, down_weight)
 
 
 def capacity_of(tok_count, experts):

time: 130 us -> 125 us (0.962)
  Pallas kernels: 126 us -> 123 us
  local copies, waits for them, and re-layouts: 3.49 us -> 2.16 us
    pallas_call x1, Pallas kernels: 126 us -> 123 us  [chained(): pl.pallas_call(functools.partial(chain_kernel, lanes, steps, cap), out_sh...]
    broadcast_in_dim x1 -> x0, local copies, waits for them, and re-layouts: 1.33 us -> none  [chained(): norm_gain[None, :]]
where the time goes in v3:
time: 125 us
  Pallas kernels  123 us (98%)
  local copies, waits for them, and re-layouts  2.16 us (2%)
    pallas_call x1, Pallas kernels, chained(): pl.pallas_call(functools.partial(chain_kernel, lanes, steps, cap), out_sh...  123 us

profile of v3, /device:TPU:0, one launch (start us, length us, event | category | flops | bytes accessed | tf_op | source)
XLA Modules:
  0.0 125.0 jit_solution(11220905360798974408)
XLA Ops:
  0.0 122.8 %shard_map.73 = bf16[128,3584]{1,0:T(8,128)(2,1)} custom-call(bf16[128,3584]{1,0:T(8,128)(2,1)} %tok_ref.1, f32[3584]{0:T(1024)} %gain_ref.1, s32[4,128]{1,0:T(4,128)} %bitcast.2, s32[4,128]{1,0:T(4,128)} %bitcast.3, bf16[1,1792,1024]{2,1,0:T(8,128)(2,1)} %gate_hbm.1, bf16[1,1792,1024]{2,1,0:T(8,128)(2,1)} %up_hbm.1, bf16[1,1024,1792]{2,1,0:T(8,128)(2,1)} %down_hbm.1), custom_call_target="tpu_custom_call" | custom-call | tf_op jit(solution)/shard_map/pallas_call | solution.py:411
  122.8 2.2 %copy.9 = bf16[128,3584]{1,0:T(8,128)(2,1)} copy(bf16[128,3584]{1,0:T(8,128)(2,1)} %shard_map.73) | data formatting | bytes 1835008
